TPU v7x, 32 devices: a whole 2x2x4 slice. The times are simulated.
32 devices in a mesh: cols: 32 (over z, y, x, core).
Axes of the slice: x: 2, y: 2, z: 4, core: 2. Of those that a mesh axis runs over, the one named last changes fastest.
Arguments:
- voxel_rows: bfloat16 [768, 32768], P(None, 'cols'), may hold values from -6 to 6
- factor_weight: bfloat16 [5, 2, 32768, 128], P(None, None, 'cols'), may hold values from -0.375 to 0.375
- extra_weight: bfloat16 [32, 128, 128], P('cols'), may hold values from -0.5 to 0.5
- extra_pairs: int32 [32, 2], replicated, may hold values from 0 to 255, as said below
- tile_owner: int32 [32], replicated, may hold values from 0 to 31, each once
Outputs:
- latent: bfloat16 [768, 32768], P(None, 'cols')
Inputs may be any that keep to these rules, and one draw needn't show every extreme that they name: `extra_pairs`: extra block k takes its column block from device k's blocks, k * 8 to (k + 1) * 8 - 1; its row block lies on a device whose index differs from k in exactly one bit. `tile_owner`: each device stores the matrix of exactly one extra block.
All inputs are finite; a program needn't handle non-finite values.
Results may differ from a plain program's by a relative error of at most 0.014.
Values may be sent and summed in bfloat16 or wider, within the bound.
A program may use at most 64 MiB of HBM per device.

v0:
```python
import jax
import jax.numpy as jnp
from jax import lax
from jax.sharding import PartitionSpec as P


def from_partner(block, axis, apart):
    count = lax.axis_size(axis)
    route = []
    for low in range(count):
        high = low | 1 << apart
        if high != low and high < count:
            route += [(low, high), (high, low)]
    return lax.ppermute(block, axis, route)


def mix_blocks(current, opposite, weights):
    row_count = current.shape[0]
    tile_width = weights.shape[2]
    blocks = weights.shape[1] // tile_width
    w_self = weights[0].reshape(blocks, tile_width, tile_width)
    w_other = weights[1].reshape(blocks, tile_width, tile_width)
    own_part = current.reshape(row_count, blocks, tile_width)
    far_part = opposite.reshape(row_count, blocks, tile_width)
    result = jnp.einsum("bia,iac->bic", own_part, w_self, preferred_element_type=jnp.float32)
    result = result + jnp.einsum(
        "bia,iac->bic", far_part, w_other, preferred_element_type=jnp.float32
    )
    return result.reshape(row_count, blocks * tile_width).astype(jnp.bfloat16)


def per_device(voxel_rows, factor_weight, extra_weight, extra_pairs, tile_owner):
    devices = lax.axis_size("cols")
    sections = devices.bit_length() - 1
    myself = lax.axis_index("cols")
    tile_width = extra_weight.shape[1]
    row_count = voxel_rows.shape[0]
    blocks = voxel_rows.shape[1] // tile_width
    bit_list = jnp.arange(sections, dtype=jnp.int32)
    bit_masks = jnp.left_shift(jnp.int32(1), bit_list)
    partners = jnp.bitwise_xor(myself, bit_masks)
    partner_rows = extra_pairs[:, 0][partners]
    usable = partner_rows // blocks == myself
    slot_table = (partner_rows - myself * blocks)[:, None] == jnp.arange(blocks, dtype=jnp.int32)[
        None, :
    ]
    placement_map = (slot_table & usable[:, None]).astype(jnp.float32)
    my_pair = extra_pairs[myself]
    my_offset = my_pair[1] - myself * blocks
    my_target = my_pair[0] // blocks
    my_bit = jnp.bitwise_xor(my_target, myself) == bit_masks
    my_block = lax.dynamic_slice_in_dim(voxel_rows, my_offset * tile_width, tile_width, 1)
    current = voxel_rows
    wanted = tile_owner[myself][None]
    shard_tiles = lax.all_gather(extra_weight, "cols", axis=0, tiled=True)
    tile_ids = jnp.arange(shard_tiles.shape[0], dtype=jnp.int32)
    matches = (tile_ids[None, :] == wanted[:, None]).astype(jnp.bfloat16)
    chosen = jnp.einsum("mn,nac->mac", matches, shard_tiles, preferred_element_type=jnp.float32)
    tile_set = chosen.astype(jnp.bfloat16)
    contrib = jnp.dot(my_block, tile_set[0], preferred_element_type=jnp.float32)
    arrivals = []
    for bit_number in range(sections):
        outgoing = jnp.where(my_bit[bit_number], contrib, jnp.zeros_like(contrib))
        arrivals.append(from_partner(outgoing, "cols", bit_number))
    incoming = jnp.stack(arrivals)
    for section_number in range(sections):
        opposite = from_partner(current, "cols", section_number)
        current = mix_blocks(current, opposite, factor_weight[section_number])
    extra_sum = jnp.einsum("sj,sbc->bjc", placement_map, incoming, precision=lax.Precision.HIGHEST)
    total = current.astype(jnp.float32) + extra_sum.reshape(row_count, blocks * tile_width)
    return total.astype(jnp.bfloat16)


def solution(mesh):
    placed = (P(None, "cols"), P(None, None, "cols", None), P("cols", None, None), P(), P())
    return jax.shard_map(
        per_device, mesh=mesh, in_specs=placed, out_specs=P(None, "cols"), check_vma=False
    )
```

profile of v0, /device:TPU:0, one launch (start us, length us, event | category | flops | bytes accessed | tf_op | source)
XLA Modules:
  0.0 227.5 jit_solution(1901442665438680729)
XLA Ops:
  6.5 0.0 all-gather.2.cloned.1.call-start
  6.5 1.7 copy.40
  8.3 0.0 copy-start
  8.3 0.5 collective-permute-start
  8.8 2.7 %fusion.31 = (bf16[1,1,1024,128]{3,2,1,0:T(8,128)(2,1)S(1)}, bf16[1,1,1024,128]{3,2,1,0:T(8,128)(2,1)}, bf16[1,1,1024,128]{3,2,1,0:T(8,128)(2,1)}, bf16[1,1,1024...) fusion(bf16[5,2,1024,128]{3,2,1,0:T(8,128)(2,1)} %param.6), kind=kLoop, calls=%fused_computation.58 | loop fusion | bytes 5242880 | tf_op jit(solution)/shard_map/slice | solution.py:22
  11.5 0.0 copy-done
  11.5 0.6 fusion.3
  12.2 0.0 collective-permute-done
  12.2 0.6 add_convert_fusion.4
  12.8 2.7 %collective-permute-start.1 = (bf16[768,1024]{0,1:T(8,128)(2,1)S(1)}, bf16[768,1024]{0,1:T(8,128)(2,1)S(1)}, u32[]{:S(2)}, u32[]{:S(2)}) collective-permute-start(bf16[768,1024]{0,1:T(8,128)(2,1)S(1)} %bitcast.96), channel_id=1, source_target_pairs={{0,2},{2,0},{1,3},{3,1},{4,6},{6,4},{5,7},{7,5},{8,10},{10,8},{9,1... | collective-permute-start | bytes 4718600 | tf_op jit(solution)/shard_map/ppermute | solution.py:14
  15.5 0.6 fusion.12
  16.1 34.3 %collective-permute-done.1 = bf16[768,1024]{0,1:T(8,128)(2,1)S(1)} collective-permute-done((bf16[768,1024]{0,1:T(8,128)(2,1)S(1)}, bf16[768,1024]{0,1:T(8,128)(2,1)S(1)}, u32[]{:S(2)}, u32[]{:S(2)}) %collective-permute-start.1) | collective-permute-done | bytes 1572896 | tf_op jit(solution)/shard_map/ppermute | solution.py:14
  50.4 0.0 copy-start.4
  50.4 0.6 add_convert_fusion.3
  51.0 1.8 collective-permute-start.2
  52.9 0.0 all-gather.2.cloned.1.call-update
  52.9 0.0 copy-done.4
  52.9 0.1 constant_dynamic-slice_fusion
  53.0 0.5 fusion.32
  55.9 0.7 fusion.33
  56.5 0.0 copy-start.3
  56.5 1.6 fusion.10
  58.2 29.9 %collective-permute-done.2 = bf16[768,1024]{0,1:T(8,128)(2,1)} collective-permute-done((bf16[768,1024]{0,1:T(8,128)(2,1)S(1)}, bf16[768,1024]{0,1:T(8,128)(2,1)}, u32[]{:S(2)}, u32[]{:S(2)}) %collective-permute-start.2) | collective-permute-done | bytes 1572896 | tf_op jit(solution)/shard_map/ppermute | solution.py:14
  88.0 0.0 copy-done.3
  88.0 0.0 copy-start.5
  88.0 2.1 add_convert_fusion.2
  90.1 1.6 collective-permute-start.3
  92.4 0.0 copy-done.5
  92.4 0.6 dynamic_slice.11
  93.0 0.6 gather_fusion
  93.6 13.9 %all-gather.2.cloned.1.call-done = bf16[32,128,128]{2,1,0:T(8,128)(2,1)} async-done(((bf16[1,128,128]{2,1,0:T(8,128)(2,1)}), bf16[32,128,128]{2,1,0:T(8,128)(2,1)}) %all-gather.2.cloned.1.call-update) | async-done | bytes 1048592 | tf_op jit(solution)/shard_map/all_gather | solution.py:55
  107.5 2.5 %fusion.14 = f32[1,128,128]{2,0,1:T(1,128)S(1)} fusion(bf16[32,128,128]{2,1,0:T(8,128)(2,1)} %all-gather.2.cloned.1.call-done, s32[]{:T(128)} %bitcast.27), kind=kOutput, calls=%fused_computation.21 | convolution fusion | flops 1048608 | bytes 1114116 | tf_op jit(solution)/shard_map/mn,nac->mac/dot_general | solution.py:58
  110.0 0.0 copy-start.2
  110.0 3.4 %broadcast_select_fusion = (f32[768,128]{1,0:T(8,128)S(1)}, f32[768,128]{1,0:T(8,128)S(1)}, f32[768,128]{1,0:T(8,128)S(1)}, f32[768,128]{1,0:T(8,128)S(1)}, f32[768,128]{1,0:T(8,128)S(1)}) fusion(pred[]{:T(512)} %bitcast.38, pred[]{:T(512)} %bitcast.36, pred[]{:T(512)} %bitcast.34, pred[]{:T(512)} %bitcast.32, pred[]{:T(512)} %bitcast.25, ...), kind=kOutput, calls=%fused_computation.28 | convolution fusion | flops 25673728 | bytes 2228233 | tf_op jit(solution)/shard_map/dot_general | solution.py:60
  113.4 0.3 collective-permute-start.5
  113.8 1.3 collective-permute-start.6
  115.1 0.8 collective-permute-start.7
  115.9 1.8 collective-permute-start.8
  117.7 0.0 collective-permute-done.5
  117.7 0.7 collective-permute-start.9
  118.4 0.0 copy-done.2
  118.5 0.0 copy-start.1
  118.5 0.6 fusion.8
  119.1 19.9 %collective-permute-done.3 = bf16[768,1024]{0,1:T(8,128)(2,1)} collective-permute-done((bf16[768,1024]{0,1:T(8,128)(2,1)S(1)}, bf16[768,1024]{0,1:T(8,128)(2,1)}, u32[]{:S(2)}, u32[]{:S(2)}) %collective-permute-start.3) | collective-permute-done | bytes 1572896 | tf_op jit(solution)/shard_map/ppermute | solution.py:14
  138.9 0.0 copy-done.1
  139.0 3.2 %add_convert_fusion.1 = bf16[8,768,128]{1,2,0:T(8,128)(2,1)} fusion(f32[8,768,128]{1,2,0:T(8,128)S(1)} %fusion.8, bf16[768,8,128]{0,2,1:T(8,128)(2,1)} %bitcast.16, bf16[8,128,128]{2,1,0:T(8,128)(2,1)S(1)} %bitcast.102), kind=kOutput, calls=%fused_computation.6 | convolution fusion | flops 202899456 | bytes 6553600 | tf_op jit(solution)/shard_map/bia,iac->bic/dot_general | solution.py:26
  142.2 1.6 collective-permute-start.4
  143.7 0.0 collective-permute-done.6
  143.8 0.0 collective-permute-done.7
  143.8 1.5 collective-permute-done.8
  145.3 1.1 collective-permute-done.9
  146.4 4.3 %fusion.1 = f32[768,128,8]{1,2,0:T(8,128)} fusion(f32[5,768,128]{2,1,0:T(8,128)S(1)} %bitcast_dynamic-update-slice_fusion, s32[5]{0:T(128)S(1)} %broadcast_subtract_fusion, pred[5]{0:T(512)(128)(4,1)S(1)} %fusion.27), kind=kOutput, calls=%fused_computation.3 | convolution fusion | flops 47186000 | bytes 5111833 | tf_op jit(solution)/shard_map/sj,sbc->bjc/dot_general | solution.py:69
  150.7 2.4 %copy.60 = f32[768,128,8]{0,1,2:T(8,128)S(1)} copy(f32[768,128,8]{1,2,0:T(8,128)} %fusion.1) | data formatting | bytes 6291456 | tf_op jit(solution)/shard_map/sj,sbc->bjc/dot_general | solution.py:69
  153.1 2.0 fusion.6
  155.1 59.3 %collective-permute-done.4 = bf16[768,1024]{0,1:T(8,128)(2,1)} collective-permute-done((bf16[768,1024]{0,1:T(8,128)(2,1)}, bf16[768,1024]{0,1:T(8,128)(2,1)}, u32[]{:S(2)}, u32[]{:S(2)}) %collective-permute-start.4) | collective-permute-done | bytes 1572896 | tf_op jit(solution)/shard_map/ppermute | solution.py:14
  214.4 2.1 add_convert_fusion
  216.5 1.6 fusion
  218.1 2.6 %copy.61 = bf16[768,1024]{1,0:T(8,128)(2,1)} copy(bf16[768,1024]{0,1:T(8,128)(2,1)} %bitcast.97) | data formatting | bytes 3145728 | tf_op jit(solution)/shard_map/convert_element_type | solution.py:71
  (11 shorter events, 0.2 us)
Async XLA Ops:
  6.5 101.0 %all-gather.2.cloned.1.call-start = ((), (), s32[]{:S(2)}) async-start(), calls=%async_computation | async-start | bytes 1081344 | tf_op jit(solution)/shard_map/all_gather | solution.py:55
  8.3 3.3 %copy-start = (bf16[768,1024]{1,0:T(8,128)(2,1)S(1)}, bf16[768,1024]{1,0:T(8,128)(2,1)}, u32[]{:S(2)}) copy-start(bf16[768,1024]{1,0:T(8,128)(2,1)} %param.5) | copy-start | bytes 4718596
  8.3 3.9 %collective-permute-start = (bf16[768,1024]{0,1:T(8,128)(2,1)S(1)}, bf16[768,1024]{0,1:T(8,128)(2,1)S(1)}, u32[]{:S(2)}, u32[]{:S(2)}) collective-permute-start(bf16[768,1024]{0,1:T(8,128)(2,1)S(1)} %copy.40), channel_id=1, source_target_pairs={{0,1},{1,0},{2,3},{3,2},{4,5},{5,4},{6,7},{7,6},{8,9},{9,8},{10,11... | collective-permute-start | bytes 4718600 | tf_op jit(solution)/shard_map/ppermute | solution.py:14
  12.8 37.6 %collective-permute-start.1 = (bf16[768,1024]{0,1:T(8,128)(2,1)S(1)}, bf16[768,1024]{0,1:T(8,128)(2,1)S(1)}, u32[]{:S(2)}, u32[]{:S(2)}) collective-permute-start(bf16[768,1024]{0,1:T(8,128)(2,1)S(1)} %bitcast.96), channel_id=1, source_target_pairs={{0,2},{2,0},{1,3},{3,1},{4,6},{6,4},{5,7},{7,5},{8,10},{10,8},{9,1... | collective-permute-start | bytes 4718600 | tf_op jit(solution)/shard_map/ppermute | solution.py:14
  50.4 2.5 %copy-start.4 = (s32[32,2]{0,1:T(2,128)S(1)}, s32[32,2]{0,1:T(2,128)}, u32[]{:S(2)}) copy-start(s32[32,2]{0,1:T(2,128)} %param.8) | copy-start | bytes 772
  51.0 37.0 %collective-permute-start.2 = (bf16[768,1024]{0,1:T(8,128)(2,1)S(1)}, bf16[768,1024]{0,1:T(8,128)(2,1)}, u32[]{:S(2)}, u32[]{:S(2)}) collective-permute-start(bf16[768,1024]{0,1:T(8,128)(2,1)S(1)} %bitcast.95), channel_id=1, source_target_pairs={{0,4},{4,0},{1,5},{5,1},{2,6},{6,2},{3,7},{7,3},{8,12},{12,8},{9,1... | collective-permute-start | bytes 4718600 | tf_op jit(solution)/shard_map/ppermute | solution.py:14
  56.5 31.5 %copy-start.3 = (bf16[1,1,1024,128]{3,2,1,0:T(8,128)(2,1)S(1)}, bf16[1,1,1024,128]{3,2,1,0:T(8,128)(2,1)}, u32[]{:S(2)}) copy-start(bf16[1,1,1024,128]{3,2,1,0:T(8,128)(2,1)} %get-tuple-element.8) | copy-start | bytes 786436
  88.0 4.4 %copy-start.5 = (s32[32]{0:T(128)S(1)}, s32[32]{0:T(128)}, u32[]{:S(2)}) copy-start(s32[32]{0:T(128)} %param.9) | copy-start | bytes 388
  90.1 48.8 %collective-permute-start.3 = (bf16[768,1024]{0,1:T(8,128)(2,1)S(1)}, bf16[768,1024]{0,1:T(8,128)(2,1)}, u32[]{:S(2)}, u32[]{:S(2)}) collective-permute-start(bf16[768,1024]{0,1:T(8,128)(2,1)S(1)} %bitcast.94), channel_id=1, source_target_pairs={{0,8},{8,0},{1,9},{9,1},{2,10},{10,2},{3,11},{11,3},{4,12},{12,4},... | collective-permute-start | bytes 4718600 | tf_op jit(solution)/shard_map/ppermute | solution.py:14
  110.0 8.4 %copy-start.2 = (bf16[1,1,1024,128]{3,2,1,0:T(8,128)(2,1)S(1)}, bf16[1,1,1024,128]{3,2,1,0:T(8,128)(2,1)}, u32[]{:S(2)}) copy-start(bf16[1,1,1024,128]{3,2,1,0:T(8,128)(2,1)} %get-tuple-element.7) | copy-start | bytes 786436
  113.4 4.3 %collective-permute-start.5 = (f32[768,128]{1,0:T(8,128)S(1)}, f32[768,128]{1,0:T(8,128)S(1)}, u32[]{:S(2)}, u32[]{:S(2)}) collective-permute-start(f32[768,128]{1,0:T(8,128)S(1)} %get-tuple-element.19), channel_id=1, source_target_pairs={{0,1},{1,0},{2,3},{3,2},{4,5},{5,4},{6,7},{7,6},{8,9},{9,8},{10,11... | collective-permute-start | bytes 1179656 | tf_op jit(solution)/shard_map/ppermute | solution.py:14
  113.8 30.0 %collective-permute-start.6 = (f32[768,128]{1,0:T(8,128)S(1)}, f32[768,128]{1,0:T(8,128)S(1)}, u32[]{:S(2)}, u32[]{:S(2)}) collective-permute-start(f32[768,128]{1,0:T(8,128)S(1)} %get-tuple-element.18), channel_id=1, source_target_pairs={{0,2},{2,0},{1,3},{3,1},{4,6},{6,4},{5,7},{7,5},{8,10},{10,8},{9,1... | collective-permute-start | bytes 1179656 | tf_op jit(solution)/shard_map/ppermute | solution.py:14
  115.1 28.7 %collective-permute-start.7 = (f32[768,128]{1,0:T(8,128)S(1)}, f32[768,128]{1,0:T(8,128)S(1)}, u32[]{:S(2)}, u32[]{:S(2)}) collective-permute-start(f32[768,128]{1,0:T(8,128)S(1)} %get-tuple-element.17), channel_id=1, source_target_pairs={{0,4},{4,0},{1,5},{5,1},{2,6},{6,2},{3,7},{7,3},{8,12},{12,8},{9,1... | collective-permute-start | bytes 1179656 | tf_op jit(solution)/shard_map/ppermute | solution.py:14
  115.9 29.4 %collective-permute-start.8 = (f32[768,128]{1,0:T(8,128)S(1)}, f32[768,128]{1,0:T(8,128)S(1)}, u32[]{:S(2)}, u32[]{:S(2)}) collective-permute-start(f32[768,128]{1,0:T(8,128)S(1)} %get-tuple-element.16), channel_id=1, source_target_pairs={{0,8},{8,0},{1,9},{9,1},{2,10},{10,2},{3,11},{11,3},{4,12},{12,4},... | collective-permute-start | bytes 1179656 | tf_op jit(solution)/shard_map/ppermute | solution.py:14
  117.7 28.7 %collective-permute-start.9 = (f32[768,128]{1,0:T(8,128)S(1)}, f32[768,128]{1,0:T(8,128)S(1)}, u32[]{:S(2)}, u32[]{:S(2)}) collective-permute-start(f32[768,128]{1,0:T(8,128)S(1)} %get-tuple-element.15), channel_id=1, source_target_pairs={{0,16},{16,0},{1,17},{17,1},{2,18},{18,2},{3,19},{19,3},{4,20},{20... | collective-permute-start | bytes 1179656 | tf_op jit(solution)/shard_map/ppermute | solution.py:14
  118.5 20.5 %copy-start.1 = (bf16[1,1,1024,128]{3,2,1,0:T(8,128)(2,1)S(1)}, bf16[1,1,1024,128]{3,2,1,0:T(8,128)(2,1)}, u32[]{:S(2)}) copy-start(bf16[1,1,1024,128]{3,2,1,0:T(8,128)(2,1)} %get-tuple-element.6) | copy-start | bytes 786436
  142.2 72.3 %collective-permute-start.4 = (bf16[768,1024]{0,1:T(8,128)(2,1)}, bf16[768,1024]{0,1:T(8,128)(2,1)}, u32[]{:S(2)}, u32[]{:S(2)}) collective-permute-start(bf16[768,1024]{0,1:T(8,128)(2,1)} %bitcast.20), channel_id=1, source_target_pairs={{0,16},{16,0},{1,17},{17,1},{2,18},{18,2},{3,19},{19,3},{4,20},{20... | collective-permute-start | bytes 4718600 | tf_op jit(solution)/shard_map/ppermute | solution.py:14
Sparse Core Ops, SparseCore 0:
  53.0 54.4 all-gather.1
where the time goes:
time: 228 us
  waiting for transfers between devices  160 us (70%)
  matrix products  24.2 us (11%)
  between operations  16.5 us (7%)
  starting transfers between devices  13.3 us (6%)
  local copies, waits for them, and re-layouts  12.1 us (5%)
    ppermute x10, waiting for transfers between devices, from_partner(): return lax.ppermute(block, axis, route)  146 us
    all_gather x1, waiting for transfers between devices, per_device(): shard_tiles = lax.all_gather(extra_weight, 'cols', axis=0, tiled=True)  13.9 us
    ppermute x10, starting transfers between devices, from_partner(): return lax.ppermute(block, axis, route)  13.2 us
    dot_general x5, matrix products, mix_blocks(): jnp.einsum('bia,iac->bic', far_part, w_other, preferred_element_type=jnp....  8.56 us
    dot_general x5, matrix products, mix_blocks(): jnp.einsum('bia,iac->bic', own_part, w_self, preferred_element_type=jnp.f...  5.5 us
  transfers between devices with their start and end apart: 11, of which 7 were waited for; matrix products, arithmetic and copies ran while one was open for 13% of the time, Pallas kernels for 0%

commit v1 on v0

v1 whole, which is shorter than its diff:
```python
import functools

import jax
import jax.numpy as jnp
from jax import lax
from jax.experimental import pallas as pl
from jax.experimental.pallas import tpu as pltpu
from jax.sharding import PartitionSpec as P

MESH = pl.DeviceIdType.MESH
ROW_PARTS = 2
VMEM_LIMIT = 58 * 1024 * 1024


def butterfly_kernel(
    sections, blocks, parts,
    vox_hbm, factor_hbm, tile_hbm, pairs, owner, out_hbm,
    vox, weights, recv, hidden, result, picked, far_picked, tiles, terms,
    vox_sem, weight_sem, tile_sem, out_sem,
    send_sem, recv_sem, pick_send, pick_recv, tile_send, tile_recv,
):
    me = lax.axis_index("cols")
    chunks, rows, width = vox.shape
    bits = [lax.rem(me // 2**b, 2) for b in range(sections)]
    partners = [me + (1 - 2 * bits[b]) * 2**b for b in range(sections)]
    last = sections - 1
    lag = list(range(last)) + [sections + 2]

    def reverse(number):
        return sum(lax.rem(number // 2**b, 2) * 2 ** (last - b) for b in range(sections))

    my_place = reverse(me)

    def window(ref, c):
        row = pl.multiple_of(lax.rem(c, parts) * rows, rows)
        col = pl.multiple_of((c // parts) * width, width)
        return ref.at[pl.ds(row, rows), pl.ds(col, width)]

    def load_vox(c):
        return pltpu.make_async_copy(window(vox_hbm, c), vox.at[c], vox_sem.at[c])

    def load_weight(s):
        return pltpu.make_async_copy(factor_hbm.at[s], weights.at[s], weight_sem.at[s])

    def store_out(c):
        return pltpu.make_async_copy(result.at[c], window(out_hbm, c), out_sem.at[c])

    def send_section(s, c):
        source = vox.at[c] if s == 0 else hidden.at[s - 1, c]
        return pltpu.make_async_remote_copy(
            src_ref=source, dst_ref=recv.at[s, c],
            send_sem=send_sem.at[s, c], recv_sem=recv_sem.at[s, c],
            device_id=(partners[s],), device_id_type=MESH,
        )

    def send_picked(b):
        return pltpu.make_async_remote_copy(
            src_ref=picked, dst_ref=far_picked.at[b],
            send_sem=pick_send.at[b], recv_sem=pick_recv.at[b],
            device_id=(partners[b],), device_id_type=MESH,
        )

    def send_tiles(g):
        start = (my_place // 2**g) * 2**g
        group = tiles.at[pl.ds(start, 2**g)]
        return pltpu.make_async_remote_copy(
            src_ref=group, dst_ref=group,
            send_sem=tile_send.at[g], recv_sem=tile_recv.at[g],
            device_id=(partners[last - g],), device_id_type=MESH,
        )

    def wait_tiles(g):
        start = (my_place // 2**g) * 2**g
        other = start + (1 - 2 * lax.rem(my_place // 2**g, 2)) * 2**g
        group = tiles.at[pl.ds(other, 2**g)]
        pltpu.make_async_remote_copy(
            src_ref=group, dst_ref=group,
            send_sem=tile_send.at[g], recv_sem=tile_recv.at[g],
            device_id=(partners[last - g],), device_id_type=MESH,
        ).wait_recv()

    tile_load = pltpu.make_async_copy(tile_hbm, tiles.at[pl.ds(my_place, 1)], tile_sem)
    for c in range(chunks):
        load_vox(c).start()
    tile_load.start()
    for s in range(sections):
        load_weight(s).start()

    barrier = pltpu.get_barrier_semaphore()
    for b in range(sections):
        pl.semaphore_signal(barrier, inc=1, device_id=(partners[b],), device_id_type=MESH)
    pl.semaphore_wait(barrier, sections)

    for c in range(chunks):
        load_vox(c).wait()
        send_section(0, c).start()
    offset = jnp.clip(pairs[me, 1] - me * blocks, 0, blocks - 1)
    for part in range(parts):
        picked[part] = vox[offset * parts + part]
    tile_load.wait()
    send_tiles(0).start()
    send_picked(last).start()
    send_picked(last - 1).start()

    pick_step = {b: 2 + b for b in range(last - 1)}
    tile_step = {g: g if g < last - 1 else g + 1 for g in range(1, sections)}

    def compute(s, c):
        i = c // parts
        if s == 0:
            own = vox[c]
        else:
            own = hidden[s - 1, c]
        both = jnp.concatenate([own, recv[s, c]], axis=1)
        place = pl.ds(pl.multiple_of(i * width, width), width)
        factors = jnp.concatenate([weights[s, 0, place, :], weights[s, 1, place, :]], axis=0)
        return jnp.dot(both, factors, preferred_element_type=jnp.float32)

    def step(t, carry):
        for s in range(sections):
            c = t - lag[s]

            @pl.when(c == 0)
            def _():
                load_weight(s).wait()

            if s == last:

                @pl.when(c == 0)
                def _():
                    wait_tiles(last)
                    for b in range(sections):
                        send_picked(b).wait_recv()
                        tile = tiles[reverse(owner[partners[b]])]
                        for part in range(parts):
                            terms[b, part] = jnp.dot(
                                far_picked[b, part], tile, preferred_element_type=jnp.float32
                            )

            @pl.when((c >= 0) & (c < chunks))
            def _():
                send_section(s, c).wait_recv()
                total = compute(s, c)
                if s < last:
                    hidden[s, c] = total.astype(jnp.bfloat16)
                    send_section(s + 1, c).start()
                else:
                    for b in range(sections):
                        slot = pairs[partners[b], 0] - me * blocks
                        mask = jnp.where(slot == c // parts, jnp.float32(1), jnp.float32(0))
                        total = total + mask * terms[b, lax.rem(c, parts)]
                    result[c] = total.astype(jnp.bfloat16)
                    store_out(c).start()

        for b, when in pick_step.items():

            @pl.when(t == when)
            def _():
                send_picked(b).start()

        for g, when in tile_step.items():

            @pl.when(t == when)
            def _():
                wait_tiles(g - 1)
                send_tiles(g).start()

        return carry

    lax.fori_loop(0, chunks + lag[last], step, 0)

    for b in range(sections):
        send_picked(b).wait_send()
        send_tiles(b).wait_send()

    def finish(c, carry):
        for s in range(sections):
            send_section(s, c).wait_send()
        store_out(c).wait()
        return carry

    lax.fori_loop(0, chunks, finish, 0)


def per_device(voxel_rows, factor_weight, extra_weight, extra_pairs, tile_owner):
    devices = lax.axis_size("cols")
    sections = devices.bit_length() - 1
    batch, columns = voxel_rows.shape
    width = extra_weight.shape[1]
    blocks = columns // width
    parts = ROW_PARTS
    rows = batch // parts
    chunks = blocks * parts
    half = jnp.bfloat16
    dma = pltpu.SemaphoreType.DMA
    anywhere = pl.BlockSpec(memory_space=pl.ANY)
    scalars = pl.BlockSpec(memory_space=pltpu.SMEM)
    return pl.pallas_call(
        functools.partial(butterfly_kernel, sections, blocks, parts),
        out_shape=jax.ShapeDtypeStruct(voxel_rows.shape, half),
        in_specs=[anywhere, anywhere, anywhere, scalars, scalars],
        out_specs=anywhere,
        scratch_shapes=[
            pltpu.VMEM((chunks, rows, width), half),
            pltpu.VMEM(factor_weight.shape, half),
            pltpu.VMEM((sections, chunks, rows, width), half),
            pltpu.VMEM((sections - 1, chunks, rows, width), half),
            pltpu.VMEM((chunks, rows, width), half),
            pltpu.VMEM((parts, rows, width), half),
            pltpu.VMEM((sections, parts, rows, width), half),
            pltpu.VMEM((devices, width, width), half),
            pltpu.VMEM((sections, parts, rows, width), jnp.float32),
            dma((chunks,)),
            dma((sections,)),
            dma,
            dma((chunks,)),
            dma((sections, chunks)),
            dma((sections, chunks)),
            dma((sections,)),
            dma((sections,)),
            dma((sections,)),
            dma((sections,)),
        ],
        compiler_params=pltpu.CompilerParams(
            collective_id=0, has_side_effects=True, vmem_limit_bytes=VMEM_LIMIT
        ),
        cost_estimate=pl.CostEstimate(
            flops=4 * sections * batch * columns * width,
            bytes_accessed=4 * batch * columns + 4 * sections * columns * width,
            transcendentals=0,
        ),
        name="butterfly",
    )(voxel_rows, factor_weight, extra_weight, extra_pairs, tile_owner)


def solution(mesh):
    placed = (P(None, "cols"), P(None, None, "cols", None), P("cols", None, None), P(), P())
    return jax.shard_map(
        per_device, mesh=mesh, in_specs=placed, out_specs=P(None, "cols"), check_vma=False
    )
```

time: 228 us -> 103 us (0.45)
  waiting for transfers between devices: 160 us -> 0 us
  Pallas kernels: 0 us -> 98.8 us
  matrix products: 24.2 us -> 0 us
  between operations: 16.5 us -> 0.01 us
  starting transfers between devices: 13.3 us -> 0 us
  local copies, waits for them, and re-layouts: 12.1 us -> 4.03 us
    ppermute x10 -> x0, waiting for transfers between devices: 146 us -> none  [from_partner(): return lax.ppermute(block, axis, route)]
    pallas_call x0 -> x1, Pallas kernels: none -> 98.8 us  [per_device(): pl.pallas_call(functools.partial(butterfly_kernel, sections, blocks, part...]
    dot_general x13 -> x0, matrix products: 24.2 us -> none  [the longest x5 8.56 us: mix_blocks(): jnp.einsum('bia,iac->bic', far_part, w_other, preferred_element_type=jnp....]
    all_gather x1 -> x0, waiting for transfers between devices: 13.9 us -> none  [per_device(): shard_tiles = lax.all_gather(extra_weight, 'cols', axis=0, tiled=True)]
    ppermute x10 -> x0, starting transfers between devices: 13.2 us -> none  [from_partner(): return lax.ppermute(block, axis, route)]
    slice x3 -> x0, local copies, waits for them, and re-layouts: 3.96 us -> none  [the longest x1 2.74 us: mix_blocks(): w_other = weights[1].reshape(blocks, tile_width, tile_width)]
    convert_element_type x1 -> x0, local copies, waits for them, and re-layouts: 2.58 us -> none  [per_device(): return total.astype(jnp.bfloat16)]
    dot_general x1 -> x0, local copies, waits for them, and re-layouts: 2.39 us -> none  [per_device(): jnp.einsum('sj,sbc->bjc', placement_map, incoming, precision=lax.Precisio...]
  transfers between devices with their start and end apart: 11 -> 0, of which waited for: 7 -> 0; matrix products, arithmetic and copies ran while one was open for 13% -> 0% of each run, Pallas kernels for 0% -> 0%
where the time goes in v1:
time: 103 us
  Pallas kernels  98.8 us (96%)
  local copies, waits for them, and re-layouts  4.03 us (4%)
    pallas_call x1, Pallas kernels, per_device(): pl.pallas_call(functools.partial(butterfly_kernel, sections, blocks, part...  98.8 us
    unnamed x2, local copies, waits for them, and re-layouts  4.03 us

profile of v1, /device:TPU:0, one launch (start us, length us, event | category | flops | bytes accessed | tf_op | source)
XLA Modules:
  0.0 102.8 jit_solution(12638007558565315396)
XLA Ops:
  0.0 1.4 %copy.6.pairs = s32[32,2]{1,0:T(8,128)} copy(s32[32,2]{0,1:T(2,128)} %param.8) | data formatting | bytes 512 | tf_op args[3]
  1.4 98.8 %butterfly.1 = bf16[768,1024]{1,0:T(8,128)(2,1)} custom-call(bf16[768,1024]{1,0:T(8,128)(2,1)} %vox_hbm.1, bf16[5,2,1024,128]{3,2,1,0:T(8,128)(2,1)} %factor_hbm.1, bf16[1,128,128]{2,1,0:T(8,128)(2,1)} %tile_hbm.1, s32[32,2]{1,0:T(8,128)} %copy.6.pairs, s32[32]{0:T(128)} %owner.1), custom_call_target="tpu_custom_call" | custom-call | flops 2013265920 | bytes 5767168 | tf_op jit(solution)/shard_map/butterfly/pallas_call | solution.py:198
  100.2 2.7 %copy.8 = bf16[768,1024]{1,0:T(8,128)(2,1)} copy(bf16[768,1024]{1,0:T(8,128)(2,1)} %butterfly.1) | data formatting | bytes 3145728

commit v2 on v1

--- a/solution.py
+++ b/solution.py
@@ -8,7 +8,7 @@
 from jax.sharding import PartitionSpec as P
 
 MESH = pl.DeviceIdType.MESH
-ROW_PARTS = 2
+ROW_PARTS = 3
 VMEM_LIMIT = 58 * 1024 * 1024
 
 
@@ -24,7 +24,8 @@
     bits = [lax.rem(me // 2**b, 2) for b in range(sections)]
     partners = [me + (1 - 2 * bits[b]) * 2**b for b in range(sections)]
     last = sections - 1
-    lag = list(range(last)) + [sections + 2]
+    pieces = [min(2 ** max(g - 1, 0), 4) for g in range(sections)]
+    lag = list(range(last)) + [sum(pieces) + 1]
 
     def reverse(number):
         return sum(lax.rem(number // 2**b, 2) * 2 ** (last - b) for b in range(sections))
@@ -53,31 +54,28 @@
             device_id=(partners[s],), device_id_type=MESH,
         )
 
-    def send_picked(b):
+    def send_picked(b, part):
         return pltpu.make_async_remote_copy(
-            src_ref=picked, dst_ref=far_picked.at[b],
-            send_sem=pick_send.at[b], recv_sem=pick_recv.at[b],
+            src_ref=picked.at[part], dst_ref=far_picked.at[b, part],
+            send_sem=pick_send.at[b, part], recv_sem=pick_recv.at[b, part],
             device_id=(partners[b],), device_id_type=MESH,
         )
 
-    def send_tiles(g):
+    def send_tiles(g, piece, arriving=False):
         start = (my_place // 2**g) * 2**g
-        group = tiles.at[pl.ds(start, 2**g)]
+        if arriving:
+            start = start + (1 - 2 * lax.rem(my_place // 2**g, 2)) * 2**g
+        count = 2**g // pieces[g]
+        group = tiles.at[pl.ds(start + piece * count, count)]
         return pltpu.make_async_remote_copy(
             src_ref=group, dst_ref=group,
-            send_sem=tile_send.at[g], recv_sem=tile_recv.at[g],
+            send_sem=tile_send.at[g, piece], recv_sem=tile_recv.at[g, piece],
             device_id=(partners[last - g],), device_id_type=MESH,
         )
 
     def wait_tiles(g):
-        start = (my_place // 2**g) * 2**g
-        other = start + (1 - 2 * lax.rem(my_place // 2**g, 2)) * 2**g
-        group = tiles.at[pl.ds(other, 2**g)]
-        pltpu.make_async_remote_copy(
-            src_ref=group, dst_ref=group,
-            send_sem=tile_send.at[g], recv_sem=tile_recv.at[g],
-            device_id=(partners[last - g],), device_id_type=MESH,
-        ).wait_recv()
+        for piece in range(pieces[g]):
+            send_tiles(g, piece, arriving=True).wait_recv()
 
     tile_load = pltpu.make_async_copy(tile_hbm, tiles.at[pl.ds(my_place, 1)], tile_sem)
     for c in range(chunks):
@@ -98,12 +96,13 @@
     for part in range(parts):
         picked[part] = vox[offset * parts + part]
     tile_load.wait()
-    send_tiles(0).start()
-    send_picked(last).start()
-    send_picked(last - 1).start()
-
-    pick_step = {b: 2 + b for b in range(last - 1)}
-    tile_step = {g: g if g < last - 1 else g + 1 for g in range(1, sections)}
+    send_tiles(0, 0).start()
+    for b in (last, last - 1):
+        for part in range(parts):
+            send_picked(b, part).start()
+
+    pick_step = {(b, part): 2 + b + 2 * part for b in range(last - 1) for part in range(parts)}
+    tile_order = [(g, piece) for g in range(1, sections) for piece in range(pieces[g])]
 
     def compute(s, c):
         i = c // parts
@@ -130,7 +129,8 @@
                 def _():
                     wait_tiles(last)
                     for b in range(sections):
-                        send_picked(b).wait_recv()
+                        for part in range(parts):
+                            send_picked(b, part).wait_recv()
                         tile = tiles[reverse(owner[partners[b]])]
                         for part in range(parts):
                             terms[b, part] = jnp.dot(
@@ -152,26 +152,29 @@
                     result[c] = total.astype(jnp.bfloat16)
                     store_out(c).start()
 
-        for b, when in pick_step.items():
+        for (b, part), when in pick_step.items():
 
             @pl.when(t == when)
             def _():
-                send_picked(b).start()
-
-        for g, when in tile_step.items():
-
-            @pl.when(t == when)
-            def _():
-                wait_tiles(g - 1)
-                send_tiles(g).start()
+                send_picked(b, part).start()
+
+        for when, (g, piece) in enumerate(tile_order):
+
+            @pl.when(t == when + 1)
+            def _():
+                if piece == 0:
+                    wait_tiles(g - 1)
+                send_tiles(g, piece).start()
 
         return carry
 
     lax.fori_loop(0, chunks + lag[last], step, 0)
 
     for b in range(sections):
-        send_picked(b).wait_send()
-        send_tiles(b).wait_send()
+        for part in range(parts):
+            send_picked(b, part).wait_send()
+        for piece in range(pieces[b]):
+            send_tiles(b, piece).wait_send()
 
     def finish(c, carry):
         for s in range(sections):
@@ -216,10 +219,10 @@
             dma((chunks,)),
             dma((sections, chunks)),
             dma((sections, chunks)),
-            dma((sections,)),
-            dma((sections,)),
-            dma((sections,)),
-            dma((sections,)),
+            dma((sections, parts)),
+            dma((sections, parts)),
+            dma((sections, 4)),
+            dma((sections, 4)),
         ],
         compiler_params=pltpu.CompilerParams(
             collective_id=0, has_side_effects=True, vmem_limit_bytes=VMEM_LIMIT

time: 103 us -> 108 us (1.049)
  Pallas kernels: 98.8 us -> 104 us
    pallas_call x1, Pallas kernels: 98.8 us -> 104 us  [per_device(): pl.pallas_call(functools.partial(butterfly_kernel, sections, blocks, part...]
where the time goes in v2:
time: 108 us
  Pallas kernels  104 us (96%)
  local copies, waits for them, and re-layouts  4.03 us (4%)
    pallas_call x1, Pallas kernels, per_device(): pl.pallas_call(functools.partial(butterfly_kernel, sections, blocks, part...  104 us
    unnamed x2, local copies, waits for them, and re-layouts  4.03 us

profile of v2, /device:TPU:0, one launch (start us, length us, event | category | flops | bytes accessed | tf_op | source)
XLA Modules:
  0.0 107.8 jit_solution(1747101673551666599)
XLA Ops:
  0.0 1.4 %copy.6.pairs = s32[32,2]{1,0:T(8,128)} copy(s32[32,2]{0,1:T(2,128)} %param.8) | data formatting | bytes 512 | tf_op args[3]
  1.4 103.7 %butterfly.1 = bf16[768,1024]{1,0:T(8,128)(2,1)} custom-call(bf16[768,1024]{1,0:T(8,128)(2,1)} %vox_hbm.1, bf16[5,2,1024,128]{3,2,1,0:T(8,128)(2,1)} %factor_hbm.1, bf16[1,128,128]{2,1,0:T(8,128)(2,1)} %tile_hbm.1, s32[32,2]{1,0:T(8,128)} %copy.6.pairs, s32[32]{0:T(128)} %owner.1), custom_call_target="tpu_custom_call" | custom-call | flops 2013265920 | bytes 5767168 | tf_op jit(solution)/shard_map/butterfly/pallas_call | solution.py:201
  105.1 2.7 %copy.8 = bf16[768,1024]{1,0:T(8,128)(2,1)} copy(bf16[768,1024]{1,0:T(8,128)(2,1)} %butterfly.1) | data formatting | bytes 3145728

commit v3 on v2

--- a/solution.py
+++ b/solution.py
@@ -26,6 +26,7 @@
     last = sections - 1
     pieces = [min(2 ** max(g - 1, 0), 4) for g in range(sections)]
     lag = list(range(last)) + [sum(pieces) + 1]
+    hold = last + 1
 
     def reverse(number):
         return sum(lax.rem(number // 2**b, 2) * 2 ** (last - b) for b in range(sections))
@@ -139,7 +140,8 @@
 
             @pl.when((c >= 0) & (c < chunks))
             def _():
-                send_section(s, c).wait_recv()
+                if s < last:
+                    send_section(s, c).wait_recv()
                 total = compute(s, c)
                 if s < last:
                     hidden[s, c] = total.astype(jnp.bfloat16)
@@ -151,6 +153,12 @@
                         total = total + mask * terms[b, lax.rem(c, parts)]
                     result[c] = total.astype(jnp.bfloat16)
                     store_out(c).start()
+
+        held = t - hold
+
+        @pl.when((held >= 0) & (held < chunks))
+        def _():
+            send_section(last, held).wait_recv()
 
         for (b, part), when in pick_step.items():
 

time: 108 us -> 109 us (level)
  no operation moved by 1% of the time
where the time goes in v3:
time: 109 us
  Pallas kernels  105 us (96%)
  local copies, waits for them, and re-layouts  4.03 us (4%)
    pallas_call x1, Pallas kernels, per_device(): pl.pallas_call(functools.partial(butterfly_kernel, sections, blocks, part...  105 us
    unnamed x2, local copies, waits for them, and re-layouts  4.03 us

profile of v3, /device:TPU:0, one launch (start us, length us, event | category | flops | bytes accessed | tf_op | source)
XLA Modules:
  0.0 108.6 jit_solution(12298927736974004467)
XLA Ops:
  0.0 1.4 %copy.6.pairs = s32[32,2]{1,0:T(8,128)} copy(s32[32,2]{0,1:T(2,128)} %param.8) | data formatting | bytes 512 | tf_op args[3]
  1.4 104.5 %butterfly.1 = bf16[768,1024]{1,0:T(8,128)(2,1)} custom-call(bf16[768,1024]{1,0:T(8,128)(2,1)} %vox_hbm.1, bf16[5,2,1024,128]{3,2,1,0:T(8,128)(2,1)} %factor_hbm.1, bf16[1,128,128]{2,1,0:T(8,128)(2,1)} %tile_hbm.1, s32[32,2]{1,0:T(8,128)} %copy.6.pairs, s32[32]{0:T(128)} %owner.1), custom_call_target="tpu_custom_call" | custom-call | flops 2013265920 | bytes 5767168 | tf_op jit(solution)/shard_map/butterfly/pallas_call | solution.py:209
  105.9 2.7 %copy.8 = bf16[768,1024]{1,0:T(8,128)(2,1)} copy(bf16[768,1024]{1,0:T(8,128)(2,1)} %butterfly.1) | data formatting | bytes 3145728

commit v4 on v2

--- a/solution.py
+++ b/solution.py
@@ -8,7 +8,7 @@
 from jax.sharding import PartitionSpec as P
 
 MESH = pl.DeviceIdType.MESH
-ROW_PARTS = 3
+ROW_PARTS = 2
 VMEM_LIMIT = 58 * 1024 * 1024
 
 
@@ -25,7 +25,8 @@
     partners = [me + (1 - 2 * bits[b]) * 2**b for b in range(sections)]
     last = sections - 1
     pieces = [min(2 ** max(g - 1, 0), 4) for g in range(sections)]
-    lag = list(range(last)) + [sum(pieces) + 1]
+    lag = list(range(last)) + [last + 1]
+    extra_step = sum(pieces) + 1
 
     def reverse(number):
         return sum(lax.rem(number // 2**b, 2) * 2 ** (last - b) for b in range(sections))
@@ -92,7 +93,7 @@
     for c in range(chunks):
         load_vox(c).wait()
         send_section(0, c).start()
-    offset = jnp.clip(pairs[me, 1] - me * blocks, 0, blocks - 1)
+    offset = jnp.clip(pairs[1, me] - me * blocks, 0, blocks - 1)
     for part in range(parts):
         picked[part] = vox[offset * parts + part]
     tile_load.wait()
@@ -115,6 +116,18 @@
         factors = jnp.concatenate([weights[s, 0, place, :], weights[s, 1, place, :]], axis=0)
         return jnp.dot(both, factors, preferred_element_type=jnp.float32)
 
+    def add_extras(total, c):
+        for b in range(sections):
+            slot = pairs[0, partners[b]] - me * blocks
+            mask = jnp.where(slot == c // parts, jnp.float32(1), jnp.float32(0))
+            total = total + mask * terms[b, lax.rem(c, parts)]
+        return total
+
+    def finish_chunk(c, carry):
+        result[c] = add_extras(result[c].astype(jnp.float32), c).astype(jnp.bfloat16)
+        store_out(c).start()
+        return carry
+
     def step(t, carry):
         for s in range(sections):
             c = t - lag[s]
@@ -123,34 +136,34 @@
             def _():
                 load_weight(s).wait()
 
-            if s == last:
-
-                @pl.when(c == 0)
-                def _():
-                    wait_tiles(last)
-                    for b in range(sections):
-                        for part in range(parts):
-                            send_picked(b, part).wait_recv()
-                        tile = tiles[reverse(owner[partners[b]])]
-                        for part in range(parts):
-                            terms[b, part] = jnp.dot(
-                                far_picked[b, part], tile, preferred_element_type=jnp.float32
-                            )
-
             @pl.when((c >= 0) & (c < chunks))
             def _():
                 send_section(s, c).wait_recv()
-                total = compute(s, c)
+                total = compute(s, c).astype(jnp.bfloat16)
                 if s < last:
-                    hidden[s, c] = total.astype(jnp.bfloat16)
+                    hidden[s, c] = total
                     send_section(s + 1, c).start()
                 else:
-                    for b in range(sections):
-                        slot = pairs[partners[b], 0] - me * blocks
-                        mask = jnp.where(slot == c // parts, jnp.float32(1), jnp.float32(0))
-                        total = total + mask * terms[b, lax.rem(c, parts)]
-                    result[c] = total.astype(jnp.bfloat16)
-                    store_out(c).start()
+                    result[c] = total
+
+        @pl.when(t == extra_step)
+        def _():
+            wait_tiles(last)
+            for b in range(sections):
+                for part in range(parts):
+                    send_picked(b, part).wait_recv()
+                tile = tiles[reverse(owner[partners[b]])]
+                for part in range(parts):
+                    terms[b, part] = jnp.dot(
+                        far_picked[b, part], tile, preferred_element_type=jnp.float32
+                    )
+            lax.fori_loop(0, min(max(extra_step - lag[last], 0), chunks), finish_chunk, 0)
+
+        c = t - lag[last]
+
+        @pl.when((t >= extra_step) & (c >= 0) & (c < chunks))
+        def _():
+            finish_chunk(c, 0)
 
         for (b, part), when in pick_step.items():
 
@@ -168,7 +181,7 @@
 
         return carry
 
-    lax.fori_loop(0, chunks + lag[last], step, 0)
+    lax.fori_loop(0, max(chunks + lag[last], extra_step + 1), step, 0)
 
     for b in range(sections):
         for part in range(parts):
@@ -233,7 +246,7 @@
             transcendentals=0,
         ),
         name="butterfly",
-    )(voxel_rows, factor_weight, extra_weight, extra_pairs, tile_owner)
+    )(voxel_rows, factor_weight, extra_weight, extra_pairs.T, tile_owner)
 
 
 def solution(mesh):

time: 108 us -> 97.5 us (0.903)
  Pallas kernels: 104 us -> 94.7 us
  local copies, waits for them, and re-layouts: 4.03 us -> 2.67 us
    pallas_call x1, Pallas kernels: 104 us -> 94.7 us  [per_device(): pl.pallas_call(functools.partial(butterfly_kernel, sections, blocks, part...]
    unnamed x2 -> x1, local copies, waits for them, and re-layouts: 4.03 us -> 2.67 us
where the time goes in v4:
time: 97.5 us; the launch traced here: 97.3 us
  Pallas kernels  94.7 us (97%)
  local copies, waits for them, and re-layouts  2.67 us (3%)
    pallas_call x1, Pallas kernels, per_device(): pl.pallas_call(functools.partial(butterfly_kernel, sections, blocks, part...  94.7 us
    unnamed x1, local copies, waits for them, and re-layouts  2.67 us

profile of v4, /device:TPU:0, one launch (start us, length us, event | category | flops | bytes accessed | tf_op | source)
XLA Modules:
  0.0 97.3 jit_solution(17069535267394865213)
XLA Ops:
  0.0 94.7 %butterfly.1 = bf16[768,1024]{1,0:T(8,128)(2,1)} custom-call(bf16[768,1024]{1,0:T(8,128)(2,1)} %vox_hbm.1, bf16[5,2,1024,128]{3,2,1,0:T(8,128)(2,1)} %factor_hbm.1, bf16[1,128,128]{2,1,0:T(8,128)(2,1)} %tile_hbm.1, s32[2,32]{1,0:T(2,128)} %bitcast.1, s32[32]{0:T(128)} %owner.1), custom_call_target="tpu_custom_call" | custom-call | flops 2013265920 | bytes 5767168 | tf_op jit(solution)/shard_map/butterfly/pallas_call | solution.py:214
  94.7 2.7 %copy.7 = bf16[768,1024]{1,0:T(8,128)(2,1)} copy(bf16[768,1024]{1,0:T(8,128)(2,1)} %butterfly.1) | data formatting | bytes 3145728

commit v5 on v4

--- a/solution.py
+++ b/solution.py
@@ -14,9 +14,9 @@
 
 def butterfly_kernel(
     sections, blocks, parts,
-    vox_hbm, factor_hbm, tile_hbm, pairs, owner, out_hbm,
-    vox, weights, recv, hidden, result, picked, far_picked, tiles, terms,
-    vox_sem, weight_sem, tile_sem, out_sem,
+    vox_hbm, factor_hbm, tile_hbm, pairs, owner, out,
+    vox, weights, recv, hidden, picked, far_picked, tiles, terms,
+    vox_sem, weight_sem, tile_sem,
     send_sem, recv_sem, pick_send, pick_recv, tile_send, tile_recv,
 ):
     me = lax.axis_index("cols")
@@ -43,9 +43,6 @@
 
     def load_weight(s):
         return pltpu.make_async_copy(factor_hbm.at[s], weights.at[s], weight_sem.at[s])
-
-    def store_out(c):
-        return pltpu.make_async_copy(result.at[c], window(out_hbm, c), out_sem.at[c])
 
     def send_section(s, c):
         source = vox.at[c] if s == 0 else hidden.at[s - 1, c]
@@ -124,8 +121,8 @@
         return total
 
     def finish_chunk(c, carry):
-        result[c] = add_extras(result[c].astype(jnp.float32), c).astype(jnp.bfloat16)
-        store_out(c).start()
+        place = window(out, c)
+        place[...] = add_extras(place[...].astype(jnp.float32), c).astype(jnp.bfloat16)
         return carry
 
     def step(t, carry):
@@ -144,7 +141,7 @@
                     hidden[s, c] = total
                     send_section(s + 1, c).start()
                 else:
-                    result[c] = total
+                    window(out, c)[...] = total
 
         @pl.when(t == extra_step)
         def _():
@@ -192,7 +189,6 @@
     def finish(c, carry):
         for s in range(sections):
             send_section(s, c).wait_send()
-        store_out(c).wait()
         return carry
 
     lax.fori_loop(0, chunks, finish, 0)
@@ -209,19 +205,18 @@
     chunks = blocks * parts
     half = jnp.bfloat16
     dma = pltpu.SemaphoreType.DMA
-    anywhere = pl.BlockSpec(memory_space=pl.ANY)
+    in_hbm = pl.BlockSpec(memory_space=pltpu.HBM)
     scalars = pl.BlockSpec(memory_space=pltpu.SMEM)
     return pl.pallas_call(
         functools.partial(butterfly_kernel, sections, blocks, parts),
-        out_shape=jax.ShapeDtypeStruct(voxel_rows.shape, half),
-        in_specs=[anywhere, anywhere, anywhere, scalars, scalars],
-        out_specs=anywhere,
+        out_shape=pltpu.VMEM(voxel_rows.shape, half),
+        in_specs=[in_hbm, in_hbm, in_hbm, scalars, scalars],
+        out_specs=pl.BlockSpec(memory_space=pltpu.VMEM),
         scratch_shapes=[
             pltpu.VMEM((chunks, rows, width), half),
             pltpu.VMEM(factor_weight.shape, half),
             pltpu.VMEM((sections, chunks, rows, width), half),
             pltpu.VMEM((sections - 1, chunks, rows, width), half),
-            pltpu.VMEM((chunks, rows, width), half),
             pltpu.VMEM((parts, rows, width), half),
             pltpu.VMEM((sections, parts, rows, width), half),
             pltpu.VMEM((devices, width, width), half),
@@ -229,7 +224,6 @@
             dma((chunks,)),
             dma((sections,)),
             dma,
-            dma((chunks,)),
             dma((sections, chunks)),
             dma((sections, chunks)),
             dma((sections, parts)),

time: 97.5 us -> 95.6 us (0.981)
  local copies, waits for them, and re-layouts: 2.67 us -> 1.15 us
    unnamed x1, local copies, waits for them, and re-layouts: 2.67 us -> 1.15 us
where the time goes in v5:
time: 95.6 us; the launch traced here: 95.4 us
  Pallas kernels  94.2 us (99%)
  local copies, waits for them, and re-layouts  1.15 us (1%)
    pallas_call x1, Pallas kernels, per_device(): pl.pallas_call(functools.partial(butterfly_kernel, sections, blocks, part...  94.2 us

profile of v5, /device:TPU:0, one launch (start us, length us, event | category | flops | bytes accessed | tf_op | source)
XLA Modules:
  0.0 95.4 jit_solution(11886092469028182143)
XLA Ops:
  0.0 94.2 %butterfly.1 = bf16[768,1024]{1,0:T(8,128)(2,1)S(1)} custom-call(bf16[768,1024]{1,0:T(8,128)(2,1)} %vox_hbm.1, bf16[5,2,1024,128]{3,2,1,0:T(8,128)(2,1)} %factor_hbm.1, bf16[1,128,128]{2,1,0:T(8,128)(2,1)} %tile_hbm.1, s32[2,32]{1,0:T(2,128)} %bitcast.1, s32[32]{0:T(128)} %owner.1), custom_call_target="tpu_custom_call" | custom-call | flops 2013265920 | bytes 5767168 | tf_op jit(solution)/shard_map/butterfly/pallas_call | solution.py:210
  94.2 1.1 %copy.7 = bf16[768,1024]{1,0:T(8,128)(2,1)} copy(bf16[768,1024]{1,0:T(8,128)(2,1)S(1)} %butterfly.1) | data formatting | bytes 3145728

commit v6 on v5

--- a/solution.py
+++ b/solution.py
@@ -9,23 +9,33 @@
 
 MESH = pl.DeviceIdType.MESH
 ROW_PARTS = 2
+MIX_STEPS = 2
+END_STEPS = 2
+WEIGHT_LEAD = 2
 VMEM_LIMIT = 58 * 1024 * 1024
 
 
 def butterfly_kernel(
     sections, blocks, parts,
     vox_hbm, factor_hbm, tile_hbm, pairs, owner, out,
-    vox, weights, recv, hidden, picked, far_picked, tiles, terms,
+    vox, weights, recv, hidden, mixed, far_mixed, ended, far_ended, far_weights,
+    picked, far_picked, tiles, terms,
     vox_sem, weight_sem, tile_sem,
-    send_sem, recv_sem, pick_send, pick_recv, tile_send, tile_recv,
+    send_sem, recv_sem, mix_send, mix_recv, end_send, end_recv, far_send, far_recv,
+    pick_send, pick_recv, tile_send, tile_recv,
 ):
     me = lax.axis_index("cols")
     chunks, rows, width = vox.shape
     bits = [lax.rem(me // 2**b, 2) for b in range(sections)]
     partners = [me + (1 - 2 * bits[b]) * 2**b for b in range(sections)]
     last = sections - 1
+    near = last - 1
+    spot = me // 2**near
+    inner = (spot == 1) | (spot == 2)
+    outer = (spot == 0) | (spot == 3)
+    mirror = me + (3 - 2 * spot) * 2**near
     pieces = [min(2 ** max(g - 1, 0), 4) for g in range(sections)]
-    lag = list(range(last)) + [last + 1]
+    mix_lag, join_lag, end_lag = near, near + MIX_STEPS, near + MIX_STEPS + END_STEPS
     extra_step = sum(pieces) + 1
 
     def reverse(number):
@@ -50,6 +60,31 @@
             src_ref=source, dst_ref=recv.at[s, c],
             send_sem=send_sem.at[s, c], recv_sem=recv_sem.at[s, c],
             device_id=(partners[s],), device_id_type=MESH,
+        )
+
+    def send_mixed(c):
+        return pltpu.make_async_remote_copy(
+            src_ref=mixed.at[c], dst_ref=far_mixed.at[c],
+            send_sem=mix_send.at[c], recv_sem=mix_recv.at[c],
+            device_id=(mirror,), device_id_type=MESH,
+        )
+
+    def send_ended(c):
+        return pltpu.make_async_remote_copy(
+            src_ref=ended.at[c], dst_ref=far_ended.at[c],
+            send_sem=end_send.at[c], recv_sem=end_recv.at[c],
+            device_id=(partners[near],), device_id_type=MESH,
+        )
+
+    def block_rows(i):
+        return pl.ds(pl.multiple_of(i * width, width), width)
+
+    def send_weight(which, i):
+        return pltpu.make_async_remote_copy(
+            src_ref=weights.at[near + which, :, block_rows(i)],
+            dst_ref=far_weights.at[which, :, block_rows(i)],
+            send_sem=far_send.at[which, i], recv_sem=far_recv.at[which, i],
+            device_id=(partners[near],), device_id_type=MESH,
         )
 
     def send_picked(b, part):
@@ -85,7 +120,8 @@
     barrier = pltpu.get_barrier_semaphore()
     for b in range(sections):
         pl.semaphore_signal(barrier, inc=1, device_id=(partners[b],), device_id_type=MESH)
-    pl.semaphore_wait(barrier, sections)
+    pl.semaphore_signal(barrier, inc=1, device_id=(mirror,), device_id_type=MESH)
+    pl.semaphore_wait(barrier, sections + 1)
 
     for c in range(chunks):
         load_vox(c).wait()
@@ -95,23 +131,26 @@
         picked[part] = vox[offset * parts + part]
     tile_load.wait()
     send_tiles(0, 0).start()
-    for b in (last, last - 1):
-        for part in range(parts):
-            send_picked(b, part).start()
-
-    pick_step = {(b, part): 2 + b + 2 * part for b in range(last - 1) for part in range(parts)}
+    for part in range(parts):
+        send_picked(last, part).start()
+    load_weight(near).wait()
+    load_weight(last).wait()
+
+    @pl.when(outer)
+    def _():
+        for i in range(min(WEIGHT_LEAD, blocks)):
+            send_weight(0, i).start()
+            send_weight(1, i).start()
+
+    pick_step = {(b, part): 2 + b + 2 * part for b in range(last) for part in range(parts)}
     tile_order = [(g, piece) for g in range(1, sections) for piece in range(pieces[g])]
 
-    def compute(s, c):
-        i = c // parts
-        if s == 0:
-            own = vox[c]
-        else:
-            own = hidden[s - 1, c]
-        both = jnp.concatenate([own, recv[s, c]], axis=1)
-        place = pl.ds(pl.multiple_of(i * width, width), width)
-        factors = jnp.concatenate([weights[s, 0, place, :], weights[s, 1, place, :]], axis=0)
-        return jnp.dot(both, factors, preferred_element_type=jnp.float32)
+    def mix(own, other, factors, c):
+        place = block_rows(c // parts)
+        both = jnp.concatenate([own, other], axis=1)
+        stack = jnp.concatenate([factors[0, place, :], factors[1, place, :]], axis=0)
+        total = jnp.dot(both, stack, preferred_element_type=jnp.float32)
+        return total.astype(jnp.bfloat16)
 
     def add_extras(total, c):
         for b in range(sections):
@@ -126,8 +165,8 @@
         return carry
 
     def step(t, carry):
-        for s in range(sections):
-            c = t - lag[s]
+        for s in range(near):
+            c = t - s
 
             @pl.when(c == 0)
             def _():
@@ -136,12 +175,60 @@
             @pl.when((c >= 0) & (c < chunks))
             def _():
                 send_section(s, c).wait_recv()
-                total = compute(s, c).astype(jnp.bfloat16)
-                if s < last:
-                    hidden[s, c] = total
+                own = vox[c] if s == 0 else hidden[s - 1, c]
+                hidden[s, c] = mix(own, recv[s, c], weights.at[s], c)
+                if s < near - 1:
                     send_section(s + 1, c).start()
                 else:
-                    window(out, c)[...] = total
+
+                    @pl.when(outer)
+                    def _():
+                        send_section(near, c).start()
+
+        c_mix = t - mix_lag
+
+        @pl.when(inner & (c_mix >= 0) & (c_mix < chunks))
+        def _():
+            c = c_mix
+            send_section(near, c).wait_recv()
+
+            @pl.when(lax.rem(c, parts) == 0)
+            def _():
+                send_weight(0, c // parts).wait_recv()
+
+            own, other = hidden[near - 1, c], recv[near, c]
+            mixed[c, 0] = mix(own, other, weights.at[near], c)
+            mixed[c, 1] = mix(other, own, far_weights.at[0], c)
+            send_mixed(c).start()
+
+        c_join = t - join_lag
+
+        @pl.when(inner & (c_join >= 0) & (c_join < chunks))
+        def _():
+            c = c_join
+            send_mixed(c).wait_recv()
+
+            @pl.when(lax.rem(c, parts) == 0)
+            def _():
+                send_weight(1, c // parts).wait_recv()
+
+            ended[c] = mix(mixed[c, 1], far_mixed[c, 0], far_weights.at[1], c)
+            send_ended(c).start()
+            window(out, c)[...] = mix(mixed[c, 0], far_mixed[c, 1], weights.at[last], c)
+
+        c_end = t - end_lag
+
+        @pl.when(outer & (c_end >= 0) & (c_end < chunks))
+        def _():
+            send_ended(c_end).wait_recv()
+            window(out, c_end)[...] = far_ended[c_end]
+
+        ahead = t // 2 + WEIGHT_LEAD
+        for which in range(2):
+
+            @pl.when(outer & (lax.rem(t, 2) == which) & (ahead < blocks))
+            def _():
+                send_weight(which, ahead).start()
 
         @pl.when(t == extra_step)
         def _():
@@ -154,13 +241,17 @@
                     terms[b, part] = jnp.dot(
                         far_picked[b, part], tile, preferred_element_type=jnp.float32
                     )
-            lax.fori_loop(0, min(max(extra_step - lag[last], 0), chunks), finish_chunk, 0)
-
-        c = t - lag[last]
-
-        @pl.when((t >= extra_step) & (c >= 0) & (c < chunks))
-        def _():
-            finish_chunk(c, 0)
+            for role, lag in ((inner, join_lag), (outer, end_lag)):
+
+                @pl.when(role)
+                def _():
+                    lax.fori_loop(0, min(max(extra_step - lag, 0), chunks), finish_chunk, 0)
+
+        for role, c in ((inner, c_join), (outer, c_end)):
+
+            @pl.when(role & (t >= extra_step) & (c >= 0) & (c < chunks))
+            def _():
+                finish_chunk(c, 0)
 
         for (b, part), when in pick_step.items():
 
@@ -178,7 +269,7 @@
 
         return carry
 
-    lax.fori_loop(0, max(chunks + lag[last], extra_step + 1), step, 0)
+    lax.fori_loop(0, max(chunks + end_lag, extra_step + 1), step, 0)
 
     for b in range(sections):
         for part in range(parts):
@@ -187,9 +278,25 @@
             send_tiles(b, piece).wait_send()
 
     def finish(c, carry):
-        for s in range(sections):
+        for s in range(near):
             send_section(s, c).wait_send()
+
+        @pl.when(outer)
+        def _():
+            send_section(near, c).wait_send()
+
+        @pl.when(inner)
+        def _():
+            send_mixed(c).wait_send()
+            send_ended(c).wait_send()
+
         return carry
+
+    @pl.when(outer)
+    def _():
+        for i in range(blocks):
+            send_weight(0, i).wait_send()
+            send_weight(1, i).wait_send()
 
     lax.fori_loop(0, chunks, finish, 0)
 
@@ -215,8 +322,13 @@
         scratch_shapes=[
             pltpu.VMEM((chunks, rows, width), half),
             pltpu.VMEM(factor_weight.shape, half),
-            pltpu.VMEM((sections, chunks, rows, width), half),
             pltpu.VMEM((sections - 1, chunks, rows, width), half),
+            pltpu.VMEM((sections - 2, chunks, rows, width), half),
+            pltpu.VMEM((chunks, 2, rows, width), half),
+            pltpu.VMEM((chunks, 2, rows, width), half),
+            pltpu.VMEM((chunks, rows, width), half),
+            pltpu.VMEM((chunks, rows, width), half),
+            pltpu.VMEM((2,) + factor_weight.shape[1:], half),
             pltpu.VMEM((parts, rows, width), half),
             pltpu.VMEM((sections, parts, rows, width), half),
             pltpu.VMEM((devices, width, width), half),
@@ -224,8 +336,14 @@
             dma((chunks,)),
             dma((sections,)),
             dma,
-            dma((sections, chunks)),
-            dma((sections, chunks)),
+            dma((sections - 1, chunks)),
+            dma((sections - 1, chunks)),
+            dma((chunks,)),
+            dma((chunks,)),
+            dma((chunks,)),
+            dma((chunks,)),
+            dma((2, blocks)),
+            dma((2, blocks)),
             dma((sections, parts)),
             dma((sections, parts)),
             dma((sections, 4)),

time: 95.6 us -> 103 us (1.077)
  Pallas kernels: 94.2 us -> 102 us
    pallas_call x1, Pallas kernels: 94.2 us -> 102 us  [per_device(): pl.pallas_call(functools.partial(butterfly_kernel, sections, blocks, part...]
where the time goes in v6:
time: 103 us
  Pallas kernels  102 us (99%)
  local copies, waits for them, and re-layouts  1.15 us (1%)
    pallas_call x1, Pallas kernels, per_device(): pl.pallas_call(functools.partial(butterfly_kernel, sections, blocks, part...  102 us

profile of v6, /device:TPU:0, one launch (start us, length us, event | category | flops | bytes accessed | tf_op | source)
XLA Modules:
  0.0 102.7 jit_solution(11047690427491603210)
XLA Ops:
  0.0 101.5 %butterfly.1 = bf16[768,1024]{1,0:T(8,128)(2,1)S(1)} custom-call(bf16[768,1024]{1,0:T(8,128)(2,1)} %vox_hbm.1, bf16[5,2,1024,128]{3,2,1,0:T(8,128)(2,1)} %factor_hbm.1, bf16[1,128,128]{2,1,0:T(8,128)(2,1)} %tile_hbm.1, s32[2,32]{1,0:T(2,128)} %bitcast.1, s32[32]{0:T(128)} %owner.1), custom_call_target="tpu_custom_call" | custom-call | flops 2013265920 | bytes 5767168 | tf_op jit(solution)/shard_map/butterfly/pallas_call | solution.py:317
  101.6 1.1 %copy.7 = bf16[768,1024]{1,0:T(8,128)(2,1)} copy(bf16[768,1024]{1,0:T(8,128)(2,1)S(1)} %butterfly.1) | data formatting | bytes 3145728

commit v7 on v5

v7 whole, which is shorter than its diff:
```python
import functools

import jax
import jax.numpy as jnp
from jax import lax
from jax.experimental import pallas as pl
from jax.experimental.pallas import tpu as pltpu
from jax.sharding import PartitionSpec as P

MESH = pl.DeviceIdType.MESH
VMEM_LIMIT = 58 * 1024 * 1024


def butterfly_kernel(
    sections, chunk_table,
    vox_hbm, factor_hbm, tile_hbm, pairs, owner, out,
    vox, weights, recv, hidden, picked, far_picked, tiles, terms,
    vox_sem, weight_sem, tile_sem,
    send_sem, recv_sem, pick_send, pick_recv, tile_send, tile_recv,
):
    me = lax.axis_index("cols")
    blocks, batch, width = vox.shape
    lead, chunks = chunk_table
    parts, half_rows = 2, batch // 2
    bits = [lax.rem(me // 2**b, 2) for b in range(sections)]
    partners = [me + (1 - 2 * bits[b]) * 2**b for b in range(sections)]
    last = sections - 1
    pieces = [min(2 ** max(g - 1, 0), 4) for g in range(sections)]
    lag = list(range(last)) + [last + 1]
    extra_step = sum(pieces) + 1

    def reverse(number):
        return sum(lax.rem(number // 2**b, 2) * 2 ** (last - b) for b in range(sections))

    my_place = reverse(me)

    def spot(c):
        if isinstance(c, int) and c < len(lead):
            return 0, sum(lead[:c]), lead[c]
        later = c - len(lead)
        block, part = 1 + later // parts, later % parts
        return block, part * half_rows, half_rows

    def window(ref, c):
        block, row, rows = spot(c)
        if not isinstance(c, int):
            row = pl.multiple_of(row, half_rows)
            block = pl.multiple_of(block * width, width)
        else:
            block = block * width
        return ref.at[pl.ds(row, rows), pl.ds(block, width)]

    def piece_of(ref, c):
        block, row, rows = spot(c)
        if not isinstance(c, int):
            row = pl.multiple_of(row, half_rows)
        return ref.at[block, pl.ds(row, rows)]

    def load_vox(c):
        return pltpu.make_async_copy(window(vox_hbm, c), piece_of(vox, c), vox_sem.at[c])

    def load_weight(s):
        return pltpu.make_async_copy(factor_hbm.at[s], weights.at[s], weight_sem.at[s])

    def send_section(s, c):
        source = vox if s == 0 else hidden.at[s - 1]
        return pltpu.make_async_remote_copy(
            src_ref=piece_of(source, c), dst_ref=piece_of(recv.at[s], c),
            send_sem=send_sem.at[s, c], recv_sem=recv_sem.at[s, c],
            device_id=(partners[s],), device_id_type=MESH,
        )

    def half_of(ref, part):
        return ref.at[pl.ds(part * half_rows, half_rows)]

    def send_picked(b, part):
        return pltpu.make_async_remote_copy(
            src_ref=half_of(picked, part), dst_ref=half_of(far_picked.at[b], part),
            send_sem=pick_send.at[b, part], recv_sem=pick_recv.at[b, part],
            device_id=(partners[b],), device_id_type=MESH,
        )

    def send_tiles(g, piece, arriving=False):
        start = (my_place // 2**g) * 2**g
        if arriving:
            start = start + (1 - 2 * lax.rem(my_place // 2**g, 2)) * 2**g
        count = 2**g // pieces[g]
        group = tiles.at[pl.ds(start + piece * count, count)]
        return pltpu.make_async_remote_copy(
            src_ref=group, dst_ref=group,
            send_sem=tile_send.at[g, piece], recv_sem=tile_recv.at[g, piece],
            device_id=(partners[last - g],), device_id_type=MESH,
        )

    def wait_tiles(g):
        for piece in range(pieces[g]):
            send_tiles(g, piece, arriving=True).wait_recv()

    tile_load = pltpu.make_async_copy(tile_hbm, tiles.at[pl.ds(my_place, 1)], tile_sem)
    for c in range(chunks):
        load_vox(c).start()
    tile_load.start()
    for s in range(sections):
        load_weight(s).start()

    barrier = pltpu.get_barrier_semaphore()
    for b in range(sections):
        pl.semaphore_signal(barrier, inc=1, device_id=(partners[b],), device_id_type=MESH)
    pl.semaphore_wait(barrier, sections)

    for c in range(chunks):
        load_vox(c).wait()
        send_section(0, c).start()
    offset = jnp.clip(pairs[1, me] - me * blocks, 0, blocks - 1)
    picked[...] = vox[offset]
    tile_load.wait()
    send_tiles(0, 0).start()
    for b in (last, last - 1):
        for part in range(parts):
            send_picked(b, part).start()

    pick_step = {(b, part): 6 + b + 2 * part for b in range(last - 1) for part in range(parts)}
    tile_order = [(g, piece) for g in range(1, sections) for piece in range(pieces[g])]

    def run_if(condition, action):
        if isinstance(condition, bool):
            if condition:
                action()
        else:
            pl.when(condition)(action)

    def mix(s, c):
        block = spot(c)[0]
        own = piece_of(vox if s == 0 else hidden.at[s - 1], c)
        both = jnp.concatenate([own[...], piece_of(recv.at[s], c)[...]], axis=1)
        place = block * width
        if not isinstance(c, int):
            place = pl.multiple_of(place, width)
        place = pl.ds(place, width)
        factors = jnp.concatenate([weights[s, 0, place, :], weights[s, 1, place, :]], axis=0)
        total = jnp.dot(both, factors, preferred_element_type=jnp.float32)
        return total.astype(jnp.bfloat16)

    def finish_chunk(c):
        block, row, rows = spot(c)
        if not isinstance(c, int):
            row = pl.multiple_of(row, half_rows)
        place = window(out, c)
        total = place[...].astype(jnp.float32)
        for b in range(sections):
            slot = pairs[0, partners[b]] - me * blocks
            mask = jnp.where(slot == block, jnp.float32(1), jnp.float32(0))
            total = total + mask * terms[b, pl.ds(row, rows), :]
        place[...] = total.astype(jnp.bfloat16)

    def start_extras():
        wait_tiles(last)
        for b in range(sections):
            for part in range(parts):
                send_picked(b, part).wait_recv()
            tile = tiles[reverse(owner[partners[b]])]
            terms[b] = jnp.dot(far_picked[b], tile, preferred_element_type=jnp.float32)
        done = min(max(extra_step - lag[last], 0), chunks)
        for c in range(min(done, len(lead))):
            finish_chunk(c)

        def finish_late(c, carry):
            finish_chunk(c)
            return carry

        lax.fori_loop(len(lead), max(done, len(lead)), finish_late, 0)

    def section_step(s, c):
        if isinstance(c, int) and c == 0:
            load_weight(s).wait()
        send_section(s, c).wait_recv()
        total = mix(s, c)
        if s < last:
            piece_of(hidden.at[s], c)[...] = total
            send_section(s + 1, c).start()
        else:
            window(out, c)[...] = total

    def tile_piece(g, piece):
        if piece == 0:
            wait_tiles(g - 1)
        send_tiles(g, piece).start()

    def step(t):
        for s in range(sections):
            c = t - lag[s]
            if isinstance(c, int):
                run_if(0 <= c < chunks, lambda: section_step(s, c))
            else:
                run_if(c < chunks, lambda: section_step(s, c))
        run_if(t == extra_step, start_extras)
        c = t - lag[last]
        if not isinstance(c, int):
            run_if((t >= extra_step) & (c < chunks), lambda: finish_chunk(c))
        for (b, part), when in pick_step.items():
            run_if(t == when, lambda: send_picked(b, part).start())
        for when, (g, piece) in enumerate(tile_order):
            run_if(t == when + 1, lambda: tile_piece(g, piece))

    def late_step(t, carry):
        step(t)
        return carry

    early = len(lead) + lag[last]
    assert early <= extra_step
    for t in range(early):
        step(t)
    lax.fori_loop(early, max(chunks + lag[last], extra_step + 1), late_step, 0)

    for b in range(sections):
        for part in range(parts):
            send_picked(b, part).wait_send()
        for piece in range(pieces[b]):
            send_tiles(b, piece).wait_send()

    def drain(c, carry=0):
        for s in range(sections):
            send_section(s, c).wait_send()
        return carry

    for c in range(len(lead)):
        drain(c)
    lax.fori_loop(len(lead), chunks, drain, 0)


def per_device(voxel_rows, factor_weight, extra_weight, extra_pairs, tile_owner):
    devices = lax.axis_size("cols")
    sections = devices.bit_length() - 1
    batch, columns = voxel_rows.shape
    width = extra_weight.shape[1]
    blocks = columns // width
    parts = 2
    lead = (batch // 8, batch // 8, batch // 4, batch // 2)
    chunks = len(lead) + (blocks - 1) * parts
    half = jnp.bfloat16
    dma = pltpu.SemaphoreType.DMA
    in_hbm = pl.BlockSpec(memory_space=pltpu.HBM)
    scalars = pl.BlockSpec(memory_space=pltpu.SMEM)
    return pl.pallas_call(
        functools.partial(butterfly_kernel, sections, (lead, chunks)),
        out_shape=pltpu.VMEM(voxel_rows.shape, half),
        in_specs=[in_hbm, in_hbm, in_hbm, scalars, scalars],
        out_specs=pl.BlockSpec(memory_space=pltpu.VMEM),
        scratch_shapes=[
            pltpu.VMEM((blocks, batch, width), half),
            pltpu.VMEM(factor_weight.shape, half),
            pltpu.VMEM((sections, blocks, batch, width), half),
            pltpu.VMEM((sections - 1, blocks, batch, width), half),
            pltpu.VMEM((batch, width), half),
            pltpu.VMEM((sections, batch, width), half),
            pltpu.VMEM((devices, width, width), half),
            pltpu.VMEM((sections, batch, width), jnp.float32),
            dma((chunks,)),
            dma((sections,)),
            dma,
            dma((sections, chunks)),
            dma((sections, chunks)),
            dma((sections, parts)),
            dma((sections, parts)),
            dma((sections, 4)),
            dma((sections, 4)),
        ],
        compiler_params=pltpu.CompilerParams(
            collective_id=0, has_side_effects=True, vmem_limit_bytes=VMEM_LIMIT
        ),
        cost_estimate=pl.CostEstimate(
            flops=4 * sections * batch * columns * width,
            bytes_accessed=4 * batch * columns + 4 * sections * columns * width,
            transcendentals=0,
        ),
        name="butterfly",
    )(voxel_rows, factor_weight, extra_weight, extra_pairs.T, tile_owner)


def solution(mesh):
    placed = (P(None, "cols"), P(None, None, "cols", None), P("cols", None, None), P(), P())
    return jax.shard_map(
        per_device, mesh=mesh, in_specs=placed, out_specs=P(None, "cols"), check_vma=False
    )
```

time: 95.6 us -> 101 us (1.056)
  Pallas kernels: 94.2 us -> 99.8 us
    pallas_call x1, Pallas kernels: 94.2 us -> 99.8 us  [per_device(): pl.pallas_call(functools.partial(butterfly_kernel, sections, (lead, chunk...]
where the time goes in v7:
time: 101 us
  Pallas kernels  99.8 us (99%)
  local copies, waits for them, and re-layouts  1.15 us (1%)
    pallas_call x1, Pallas kernels, per_device(): pl.pallas_call(functools.partial(butterfly_kernel, sections, (lead, chunk...  99.8 us

profile of v7, /device:TPU:0, one launch (start us, length us, event | category | flops | bytes accessed | tf_op | source)
XLA Modules:
  0.0 101.0 jit_solution(13058466919096670198)
XLA Ops:
  0.0 99.8 %butterfly.1 = bf16[768,1024]{1,0:T(8,128)(2,1)S(1)} custom-call(bf16[768,1024]{1,0:T(8,128)(2,1)} %vox_hbm.1, bf16[5,2,1024,128]{3,2,1,0:T(8,128)(2,1)} %factor_hbm.1, bf16[1,128,128]{2,1,0:T(8,128)(2,1)} %tile_hbm.1, s32[2,32]{1,0:T(2,128)} %bitcast.1, s32[32]{0:T(128)} %owner.1), custom_call_target="tpu_custom_call" | custom-call | flops 2013265920 | bytes 5767168 | tf_op jit(solution)/shard_map/butterfly/pallas_call | solution.py:244
  99.8 1.1 %copy.7 = bf16[768,1024]{1,0:T(8,128)(2,1)} copy(bf16[768,1024]{1,0:T(8,128)(2,1)S(1)} %butterfly.1) | data formatting | bytes 3145728

commit v8 on v5

--- a/solution.py
+++ b/solution.py
@@ -15,17 +15,16 @@
 def butterfly_kernel(
     sections, blocks, parts,
     vox_hbm, factor_hbm, tile_hbm, pairs, owner, out,
-    vox, weights, recv, hidden, picked, far_picked, tiles, terms,
+    acts, weights, recv, picked, far_picked, tiles, terms,
     vox_sem, weight_sem, tile_sem,
     send_sem, recv_sem, pick_send, pick_recv, tile_send, tile_recv,
 ):
     me = lax.axis_index("cols")
-    chunks, rows, width = vox.shape
+    _, chunks, rows, width = acts.shape
     bits = [lax.rem(me // 2**b, 2) for b in range(sections)]
     partners = [me + (1 - 2 * bits[b]) * 2**b for b in range(sections)]
     last = sections - 1
     pieces = [min(2 ** max(g - 1, 0), 4) for g in range(sections)]
-    lag = list(range(last)) + [last + 1]
     extra_step = sum(pieces) + 1
 
     def reverse(number):
@@ -39,17 +38,17 @@
         return ref.at[pl.ds(row, rows), pl.ds(col, width)]
 
     def load_vox(c):
-        return pltpu.make_async_copy(window(vox_hbm, c), vox.at[c], vox_sem.at[c])
+        return pltpu.make_async_copy(window(vox_hbm, c), acts.at[0, c], vox_sem.at[c])
 
     def load_weight(s):
         return pltpu.make_async_copy(factor_hbm.at[s], weights.at[s], weight_sem.at[s])
 
-    def send_section(s, c):
-        source = vox.at[c] if s == 0 else hidden.at[s - 1, c]
+    def send_section(s, c, stride):
+        partner = me + (1 - 2 * lax.rem(me // stride, 2)) * stride
         return pltpu.make_async_remote_copy(
-            src_ref=source, dst_ref=recv.at[s, c],
+            src_ref=acts.at[s, c], dst_ref=recv.at[s, c],
             send_sem=send_sem.at[s, c], recv_sem=recv_sem.at[s, c],
-            device_id=(partners[s],), device_id_type=MESH,
+            device_id=(partner,), device_id_type=MESH,
         )
 
     def send_picked(b, part):
@@ -76,8 +75,12 @@
             send_tiles(g, piece, arriving=True).wait_recv()
 
     tile_load = pltpu.make_async_copy(tile_hbm, tiles.at[pl.ds(my_place, 1)], tile_sem)
-    for c in range(chunks):
+
+    def start_load(c, carry):
         load_vox(c).start()
+        return carry
+
+    lax.fori_loop(0, chunks, start_load, 0)
     tile_load.start()
     for s in range(sections):
         load_weight(s).start()
@@ -87,12 +90,15 @@
         pl.semaphore_signal(barrier, inc=1, device_id=(partners[b],), device_id_type=MESH)
     pl.semaphore_wait(barrier, sections)
 
-    for c in range(chunks):
+    def send_first(c, carry):
         load_vox(c).wait()
-        send_section(0, c).start()
+        send_section(0, c, 1).start()
+        return carry
+
+    lax.fori_loop(0, chunks, send_first, 0)
     offset = jnp.clip(pairs[1, me] - me * blocks, 0, blocks - 1)
     for part in range(parts):
-        picked[part] = vox[offset * parts + part]
+        picked[part] = acts[0, offset * parts + part]
     tile_load.wait()
     send_tiles(0, 0).start()
     for b in (last, last - 1):
@@ -102,32 +108,33 @@
     pick_step = {(b, part): 2 + b + 2 * part for b in range(last - 1) for part in range(parts)}
     tile_order = [(g, piece) for g in range(1, sections) for piece in range(pieces[g])]
 
-    def compute(s, c):
-        i = c // parts
-        if s == 0:
-            own = vox[c]
-        else:
-            own = hidden[s - 1, c]
-        both = jnp.concatenate([own, recv[s, c]], axis=1)
-        place = pl.ds(pl.multiple_of(i * width, width), width)
+    def mix(s, c):
+        both = jnp.concatenate([acts[s, c], recv[s, c]], axis=1)
+        place = pl.ds(pl.multiple_of((c // parts) * width, width), width)
         factors = jnp.concatenate([weights[s, 0, place, :], weights[s, 1, place, :]], axis=0)
-        return jnp.dot(both, factors, preferred_element_type=jnp.float32)
-
-    def add_extras(total, c):
+        total = jnp.dot(both, factors, preferred_element_type=jnp.float32)
+        return total.astype(jnp.bfloat16)
+
+    def finish_chunk(c, carry):
+        total = acts[sections, c].astype(jnp.float32)
         for b in range(sections):
             slot = pairs[0, partners[b]] - me * blocks
             mask = jnp.where(slot == c // parts, jnp.float32(1), jnp.float32(0))
             total = total + mask * terms[b, lax.rem(c, parts)]
-        return total
-
-    def finish_chunk(c, carry):
-        place = window(out, c)
-        place[...] = add_extras(place[...].astype(jnp.float32), c).astype(jnp.bfloat16)
+        window(out, c)[...] = total.astype(jnp.bfloat16)
+        return carry
+
+    def make_term(index, carry):
+        b, part = index // parts, lax.rem(index, parts)
+        tile = tiles[carry[0]]
+        for other in range(1, sections):
+            tile = jnp.where(b == other, tiles[carry[other]], tile)
+        terms[b, part] = jnp.dot(far_picked[b, part], tile, preferred_element_type=jnp.float32)
         return carry
 
     def step(t, carry):
-        for s in range(sections):
-            c = t - lag[s]
+        def section(s, stride):
+            c = t - s - jnp.where(s == last, 1, 0)
 
             @pl.when(c == 0)
             def _():
@@ -135,13 +142,16 @@
 
             @pl.when((c >= 0) & (c < chunks))
             def _():
-                send_section(s, c).wait_recv()
-                total = compute(s, c).astype(jnp.bfloat16)
-                if s < last:
-                    hidden[s, c] = total
-                    send_section(s + 1, c).start()
-                else:
-                    window(out, c)[...] = total
+                send_section(s, c, stride).wait_recv()
+                acts[s + 1, c] = mix(s, c)
+
+                @pl.when(s < last)
+                def _():
+                    send_section(s + 1, c, 2 * stride).start()
+
+            return 2 * stride
+
+        lax.fori_loop(0, sections, section, 1)
 
         @pl.when(t == extra_step)
         def _():
@@ -149,18 +159,13 @@
             for b in range(sections):
                 for part in range(parts):
                     send_picked(b, part).wait_recv()
-                tile = tiles[reverse(owner[partners[b]])]
-                for part in range(parts):
-                    terms[b, part] = jnp.dot(
-                        far_picked[b, part], tile, preferred_element_type=jnp.float32
-                    )
-            lax.fori_loop(0, min(max(extra_step - lag[last], 0), chunks), finish_chunk, 0)
-
-        c = t - lag[last]
-
-        @pl.when((t >= extra_step) & (c >= 0) & (c < chunks))
-        def _():
-            finish_chunk(c, 0)
+            wanted = tuple(reverse(owner[partners[b]]) for b in range(sections))
+            lax.fori_loop(0, sections * parts, make_term, wanted)
+
+        done = t - sections
+        begin = jnp.where(t == extra_step, 0, done)
+        stop = jnp.where(t >= extra_step, jnp.minimum(done + 1, chunks), begin)
+        lax.fori_loop(begin, stop, finish_chunk, 0)
 
         for (b, part), when in pick_step.items():
 
@@ -178,7 +183,7 @@
 
         return carry
 
-    lax.fori_loop(0, max(chunks + lag[last], extra_step + 1), step, 0)
+    lax.fori_loop(0, max(chunks + sections, extra_step + 1), step, 0)
 
     for b in range(sections):
         for part in range(parts):
@@ -186,12 +191,15 @@
         for piece in range(pieces[b]):
             send_tiles(b, piece).wait_send()
 
-    def finish(c, carry):
-        for s in range(sections):
-            send_section(s, c).wait_send()
-        return carry
-
-    lax.fori_loop(0, chunks, finish, 0)
+    def drain(c, carry):
+        def one(s, stride):
+            send_section(s, c, stride).wait_send()
+            return 2 * stride
+
+        lax.fori_loop(0, sections, one, 1)
+        return carry
+
+    lax.fori_loop(0, chunks, drain, 0)
 
 
 def per_device(voxel_rows, factor_weight, extra_weight, extra_pairs, tile_owner):
@@ -213,10 +221,9 @@
         in_specs=[in_hbm, in_hbm, in_hbm, scalars, scalars],
         out_specs=pl.BlockSpec(memory_space=pltpu.VMEM),
         scratch_shapes=[
-            pltpu.VMEM((chunks, rows, width), half),
+            pltpu.VMEM((sections + 1, chunks, rows, width), half),
             pltpu.VMEM(factor_weight.shape, half),
             pltpu.VMEM((sections, chunks, rows, width), half),
-            pltpu.VMEM((sections - 1, chunks, rows, width), half),
             pltpu.VMEM((parts, rows, width), half),
             pltpu.VMEM((sections, parts, rows, width), half),
             pltpu.VMEM((devices, width, width), half),

time: 95.6 us -> 96.5 us (level)
  Pallas kernels: 94.2 us -> 95.2 us
where the time goes in v8:
time: 96.5 us; the launch traced here: 96.3 us
  Pallas kernels  95.2 us (99%)
  local copies, waits for them, and re-layouts  1.15 us (1%)
    pallas_call x1, Pallas kernels, per_device(): pl.pallas_call(functools.partial(butterfly_kernel, sections, blocks, part...  95.2 us

profile of v8, /device:TPU:0, one launch (start us, length us, event | category | flops | bytes accessed | tf_op | source)
XLA Modules:
  0.0 96.3 jit_solution(17263171116230984019)
XLA Ops:
  0.0 95.2 %butterfly.1 = bf16[768,1024]{1,0:T(8,128)(2,1)S(1)} custom-call(bf16[768,1024]{1,0:T(8,128)(2,1)} %vox_hbm.1, bf16[5,2,1024,128]{3,2,1,0:T(8,128)(2,1)} %factor_hbm.1, bf16[1,128,128]{2,1,0:T(8,128)(2,1)} %tile_hbm.1, s32[2,32]{1,0:T(2,128)} %bitcast.1, s32[32]{0:T(128)} %owner.1), custom_call_target="tpu_custom_call" | custom-call | flops 2013265920 | bytes 5767168 | tf_op jit(solution)/shard_map/butterfly/pallas_call | solution.py:218
  95.2 1.1 %copy.7 = bf16[768,1024]{1,0:T(8,128)(2,1)} copy(bf16[768,1024]{1,0:T(8,128)(2,1)S(1)} %butterfly.1) | data formatting | bytes 3145728

commit v9 on v5

--- a/solution.py
+++ b/solution.py
@@ -9,6 +9,7 @@
 
 MESH = pl.DeviceIdType.MESH
 ROW_PARTS = 2
+FIRST_LEAD = 2
 VMEM_LIMIT = 58 * 1024 * 1024
 
 
@@ -89,6 +90,7 @@
 
     for c in range(chunks):
         load_vox(c).wait()
+    for c in range(min(FIRST_LEAD, chunks)):
         send_section(0, c).start()
     offset = jnp.clip(pairs[1, me] - me * blocks, 0, blocks - 1)
     for part in range(parts):
@@ -126,6 +128,10 @@
         return carry
 
     def step(t, carry):
+        @pl.when(t + FIRST_LEAD < chunks)
+        def _():
+            send_section(0, t + FIRST_LEAD).start()
+
         for s in range(sections):
             c = t - lag[s]
 

time: 95.6 us -> 95.6 us (level)
  no operation moved by 1% of the time
where the time goes in v9:
time: 95.6 us; the launch traced here: 95.4 us
  Pallas kernels  94.3 us (99%)
  local copies, waits for them, and re-layouts  1.15 us (1%)
    pallas_call x1, Pallas kernels, per_device(): pl.pallas_call(functools.partial(butterfly_kernel, sections, blocks, part...  94.3 us

profile of v9, /device:TPU:0, one launch (start us, length us, event | category | flops | bytes accessed | tf_op | source)
XLA Modules:
  0.0 95.4 jit_solution(278527277047350965)
XLA Ops:
  0.0 94.3 %butterfly.1 = bf16[768,1024]{1,0:T(8,128)(2,1)S(1)} custom-call(bf16[768,1024]{1,0:T(8,128)(2,1)} %vox_hbm.1, bf16[5,2,1024,128]{3,2,1,0:T(8,128)(2,1)} %factor_hbm.1, bf16[1,128,128]{2,1,0:T(8,128)(2,1)} %tile_hbm.1, s32[2,32]{1,0:T(2,128)} %bitcast.1, s32[32]{0:T(128)} %owner.1), custom_call_target="tpu_custom_call" | custom-call | flops 2013265920 | bytes 5767168 | tf_op jit(solution)/shard_map/butterfly/pallas_call | solution.py:216
  94.3 1.1 %copy.7 = bf16[768,1024]{1,0:T(8,128)(2,1)} copy(bf16[768,1024]{1,0:T(8,128)(2,1)S(1)} %butterfly.1) | data formatting | bytes 3145728

commit v10 on v9

--- a/solution.py
+++ b/solution.py
@@ -8,7 +8,7 @@
 from jax.sharding import PartitionSpec as P
 
 MESH = pl.DeviceIdType.MESH
-ROW_PARTS = 2
+ROW_PARTS = 3
 FIRST_LEAD = 2
 VMEM_LIMIT = 58 * 1024 * 1024
 
@@ -26,7 +26,7 @@
     partners = [me + (1 - 2 * bits[b]) * 2**b for b in range(sections)]
     last = sections - 1
     pieces = [min(2 ** max(g - 1, 0), 4) for g in range(sections)]
-    lag = list(range(last)) + [last + 1]
+    lag = list(range(last - 1)) + [last, last + 2]
     extra_step = sum(pieces) + 1
 
     def reverse(number):

time: 95.6 us -> 103 us (1.077)
  Pallas kernels: 94.3 us -> 102 us
    pallas_call x1, Pallas kernels: 94.3 us -> 102 us  [per_device(): pl.pallas_call(functools.partial(butterfly_kernel, sections, blocks, part...]
where the time goes in v10:
time: 103 us
  Pallas kernels  102 us (99%)
  local copies, waits for them, and re-layouts  1.15 us (1%)
    pallas_call x1, Pallas kernels, per_device(): pl.pallas_call(functools.partial(butterfly_kernel, sections, blocks, part...  102 us

profile of v10, /device:TPU:0, one launch (start us, length us, event | category | flops | bytes accessed | tf_op | source)
XLA Modules:
  0.0 102.7 jit_solution(15921776934781390413)
XLA Ops:
  0.0 101.6 %butterfly.1 = bf16[768,1024]{1,0:T(8,128)(2,1)S(1)} custom-call(bf16[768,1024]{1,0:T(8,128)(2,1)} %vox_hbm.1, bf16[5,2,1024,128]{3,2,1,0:T(8,128)(2,1)} %factor_hbm.1, bf16[1,128,128]{2,1,0:T(8,128)(2,1)} %tile_hbm.1, s32[2,32]{1,0:T(2,128)} %bitcast.1, s32[32]{0:T(128)} %owner.1), custom_call_target="tpu_custom_call" | custom-call | flops 2013265920 | bytes 5767168 | tf_op jit(solution)/shard_map/butterfly/pallas_call | solution.py:216
  101.6 1.1 %copy.7 = bf16[768,1024]{1,0:T(8,128)(2,1)} copy(bf16[768,1024]{1,0:T(8,128)(2,1)S(1)} %butterfly.1) | data formatting | bytes 3145728

commit v11 on v9

--- a/solution.py
+++ b/solution.py
@@ -26,7 +26,7 @@
     partners = [me + (1 - 2 * bits[b]) * 2**b for b in range(sections)]
     last = sections - 1
     pieces = [min(2 ** max(g - 1, 0), 4) for g in range(sections)]
-    lag = list(range(last)) + [last + 1]
+    lag = list(range(sections))
     extra_step = sum(pieces) + 1
 
     def reverse(number):

time: 95.6 us -> 98.2 us (1.027)
  Pallas kernels: 94.3 us -> 96.9 us
    pallas_call x1, Pallas kernels: 94.3 us -> 96.9 us  [per_device(): pl.pallas_call(functools.partial(butterfly_kernel, sections, blocks, part...]
where the time goes in v11:
time: 98.2 us; the launch traced here: 98.1 us
  Pallas kernels  96.9 us (99%)
  local copies, waits for them, and re-layouts  1.15 us (1%)
    pallas_call x1, Pallas kernels, per_device(): pl.pallas_call(functools.partial(butterfly_kernel, sections, blocks, part...  96.9 us

profile of v11, /device:TPU:0, one launch (start us, length us, event | category | flops | bytes accessed | tf_op | source)
XLA Modules:
  0.0 98.1 jit_solution(1069611629343825914)
XLA Ops:
  0.0 96.9 %butterfly.1 = bf16[768,1024]{1,0:T(8,128)(2,1)S(1)} custom-call(bf16[768,1024]{1,0:T(8,128)(2,1)} %vox_hbm.1, bf16[5,2,1024,128]{3,2,1,0:T(8,128)(2,1)} %factor_hbm.1, bf16[1,128,128]{2,1,0:T(8,128)(2,1)} %tile_hbm.1, s32[2,32]{1,0:T(2,128)} %bitcast.1, s32[32]{0:T(128)} %owner.1), custom_call_target="tpu_custom_call" | custom-call | flops 2013265920 | bytes 5767168 | tf_op jit(solution)/shard_map/butterfly/pallas_call | solution.py:216
  96.9 1.1 %copy.7 = bf16[768,1024]{1,0:T(8,128)(2,1)} copy(bf16[768,1024]{1,0:T(8,128)(2,1)S(1)} %butterfly.1) | data formatting | bytes 3145728
